TPU v7x, 32 devices: a whole 2x2x4 slice. The times are simulated.
32 devices in a mesh: ex: 8 (over z, y), hg: 4 (over x, core).
Axes of the slice: x: 2, y: 2, z: 4, core: 2. Of those that a mesh axis runs over, the one named last changes fastest.
Arguments:
- residual_in: bfloat16 [64, 2048], P('ex'), may hold values from -3 to 3
- queries: bfloat16 [64, 16, 576], P('ex', 'hg'), may hold values from -6 to 6
- new_latent: bfloat16 [64, 576], P('ex'), may hold values from -4 to 4
- cache: bfloat16 [64, 240, 576], P('ex'), may hold values from -4 to 4
- lengths: int32 [64], P('ex'), may hold values from 2 to 240, as said below
- value_up: bfloat16 [16, 512, 128], P('hg'), may hold values from -0.25 to 0.25
- out_proj: bfloat16 [16, 128, 2048], P('hg'), may hold values from -0.125 to 0.125
- norm_gain: float32 [2048], replicated, may hold values from 0.1 to 1.9
- routes: int32 [64, 6], P('ex'), may hold values from 0 to 63, as said below
- gate_weights: float32 [64, 6], P('ex'), may hold values from 0.05 to 0.6
- expert_gate_up: bfloat16 [64, 2, 1408, 2048], P('ex', None, 'hg'), may hold values from -0.125 to 0.125
- expert_down: bfloat16 [64, 1408, 2048], P('ex', 'hg'), may hold values from -0.15625 to 0.15625
- shared_gate_up: bfloat16 [2, 1408, 2048], P(None, 'hg'), may hold values from -0.125 to 0.125
- shared_down: bfloat16 [1408, 2048], P('hg'), may hold values from -0.15625 to 0.15625
Outputs:
- attended: bfloat16 [64, 2048], P('ex', 'hg')
- layer_out: bfloat16 [64, 2048], P('ex', 'hg')
Inputs may be any that keep to these rules, and one draw needn't show every extreme that they name: `lengths`: some row has exactly 240 cached tokens. `routes`: each row names 6 different experts; the 8 rows of one device (aligned blocks of rows) name any one expert at most 2 times.
All inputs are finite; a program needn't handle non-finite values.
Results may differ from a plain program's by a relative error of at most 0.009.
Values may be sent and summed in bfloat16 or wider, within the bound.
A program may use at most 128 MiB of HBM per device.

v0:
```python
import jax
import jax.numpy as jnp
from jax import lax
from jax.sharding import PartitionSpec as P

LATENT = 512
ROPE = 64
QK_NOPE = 128
EXPERTS = 64
CAP = 2


norm_eps = 1e-06


def attend_heads(queries, new_latent, cache, lengths, value_up, out_proj):
    score_scale = (QK_NOPE + ROPE) ** (-0.5)
    scores = (
        jnp.einsum("rhk,rtk->rht", queries, cache, preferred_element_type=jnp.float32) * score_scale
    )
    own_score = (
        jnp.einsum("rhk,rk->rh", queries, new_latent, preferred_element_type=jnp.float32)
        * score_scale
    )
    usable = jnp.arange(cache.shape[1])[None, None, :] < lengths[:, None, None]
    scores = jnp.where(usable, scores, -jnp.inf)
    peak = jnp.maximum(jnp.max(scores, axis=2), own_score)
    weights_cache = jnp.where(usable, jnp.exp(scores - peak[:, :, None]), 0.0)
    weight_own = jnp.exp(own_score - peak)
    denominator = jnp.sum(weights_cache, axis=2) + weight_own
    weights_bf = (weights_cache / denominator[:, :, None]).astype(jnp.bfloat16)
    own_bf = (weight_own / denominator).astype(jnp.bfloat16)
    latent_mix = jnp.einsum(
        "rht,rtl->rhl", weights_bf, cache[:, :, :LATENT], preferred_element_type=jnp.float32
    )
    latent_mix = latent_mix + own_bf.astype(jnp.float32)[:, :, None] * new_latent[
        :, None, :LATENT
    ].astype(jnp.float32)
    head_out = jnp.einsum(
        "rhl,hlv->rhv",
        latent_mix.astype(jnp.bfloat16),
        value_up,
        preferred_element_type=jnp.float32,
    ).astype(jnp.bfloat16)
    return jnp.einsum("rhv,hvd->rd", head_out, out_proj, preferred_element_type=jnp.float32)


def slot_places(routes):
    flat_routes = routes.reshape(-1)
    matches = (flat_routes[:, None] == jnp.arange(EXPERTS, dtype=jnp.int32)[None, :]).astype(
        jnp.int32
    )
    before = jnp.cumsum(matches, axis=0) - matches
    slot_rank = jnp.sum(before * matches, axis=1)
    target = flat_routes * CAP + slot_rank
    return target[:, None] == jnp.arange(EXPERTS * CAP, dtype=jnp.int32)[None, :]


def run_experts(arrived, gate_up, down_proj):
    pair_in = jnp.einsum("necd,ejfd->jnecf", arrived, gate_up, preferred_element_type=jnp.float32)
    activation = (jax.nn.silu(pair_in[0]) * pair_in[1]).astype(jnp.bfloat16)
    return jnp.einsum("necf,efd->necd", activation, down_proj, preferred_element_type=jnp.float32)


def local(
    residual_in,
    queries,
    new_latent,
    cache,
    lengths,
    value_up,
    out_proj,
    norm_gain,
    routes,
    gate_weights,
    expert_gate_up,
    expert_down,
    shared_gate_up,
    shared_down,
):
    rows_here, top_k = routes.shape
    model_width = residual_in.shape[1]
    groups = lax.axis_size("hg")
    owners = lax.axis_size("ex")
    quarter = model_width // groups
    offset = lax.axis_index("hg") * quarter
    attn_part = attend_heads(queries, new_latent, cache, lengths, value_up, out_proj)
    attn_total = lax.psum(attn_part, "hg")
    hidden_state = residual_in.astype(jnp.float32) + attn_total
    inverse = lax.rsqrt(jnp.mean(hidden_state * hidden_state, axis=1) + norm_eps)
    normed = (hidden_state * inverse[:, None] * norm_gain).astype(jnp.bfloat16)
    state_share = lax.dynamic_slice_in_dim(hidden_state, offset, quarter, 1)
    places = slot_places(routes)
    senders = jnp.sum(places.reshape(rows_here, top_k, -1).astype(jnp.int32), axis=1).astype(
        jnp.bfloat16
    )
    outgoing = jnp.einsum("rs,rd->sd", senders, normed, preferred_element_type=jnp.float32).astype(
        jnp.bfloat16
    )
    outgoing = outgoing.reshape(owners, expert_down.shape[0], CAP, normed.shape[1])
    returned_part = lax.all_to_all(
        run_experts(
            lax.all_to_all(outgoing, "ex", split_axis=0, concat_axis=0, tiled=True),
            expert_gate_up,
            expert_down,
        ),
        "ex",
        split_axis=0,
        concat_axis=0,
        tiled=True,
    )
    shared_pair = jnp.einsum(
        "rd,jfd->jrf", normed, shared_gate_up, preferred_element_type=jnp.float32
    )
    shared_act = (jax.nn.silu(shared_pair[0]) * shared_pair[1]).astype(jnp.bfloat16)
    shared_part = jnp.dot(shared_act, shared_down, preferred_element_type=jnp.float32)
    back_flat = returned_part.reshape(EXPERTS * CAP, -1)
    picked = jnp.dot(places.astype(jnp.float32), back_flat, precision=lax.Precision.HIGHEST)
    stacked = jnp.concatenate(
        [picked.reshape(rows_here, top_k, model_width), shared_part[:, None, :]], axis=1
    )
    summed_all = lax.psum_scatter(stacked, "hg", scatter_dimension=2, tiled=True)
    rounded = lax.optimization_barrier(summed_all[:, :top_k].astype(jnp.bfloat16))
    expert_out = rounded.astype(jnp.float32)
    shared_out = summed_all[:, top_k]
    weighted = jnp.sum(gate_weights[:, :, None] * expert_out, axis=1)
    layer_out = (state_share + shared_out + weighted).astype(jnp.bfloat16)
    return (state_share.astype(jnp.bfloat16), layer_out)


def solution(mesh):
    placed = (
        P("ex", None),
        P("ex", "hg", None),
        P("ex", None),
        P("ex", None, None),
        P("ex"),
        P("hg", None, None),
        P("hg", None, None),
        P(),
        P("ex", None),
        P("ex", None),
        P("ex", None, "hg", None),
        P("ex", "hg", None),
        P(None, "hg", None),
        P("hg", None),
    )
    return jax.shard_map(
        local, mesh=mesh, in_specs=placed, out_specs=(P("ex", "hg"), P("ex", "hg")), check_vma=False
    )
```

profile of v0, /device:TPU:0, one launch (start us, length us, event | category | flops | bytes accessed | tf_op | source)
XLA Modules:
  0.0 153.3 jit_solution(14524793073974552776)
XLA Ops:
  7.2 0.0 copy-start
  7.2 0.0 all-reduce.2.cloned.1.call-start
  7.2 0.0 copy-start.1
  7.2 0.9 iota_compare_fusion.3
  8.1 0.8 slice_convert_fusion.1
  9.0 0.9 fusion.33
  9.9 0.0 copy-start.3
  9.9 2.3 %fusion.53 = (f32[8,4]{1,0:T(8,128)S(1)}, f32[8,4,240]{2,1,0:T(4,128)S(1)}) fusion(bf16[8,4,576]{2,1,0:T(4,128)(2,1)} %param.15, bf16[8,240,576]{1,2,0:T(8,128)(2,1)} %param.17, pred[8,240]{1,0:T(8,128)(4,1)S(1)} %iota_compare_fusion.3), kind=kOutput, calls=%fused_computation.73 | convolution fusion | flops 8870368 | bytes 2281472 | tf_op jit(solution)/shard_map/rhk,rtk->rht/dot_general | solution.py:19
  12.2 0.2 fusion.32
  12.4 0.0 copy-done.1
  12.4 0.0 copy-start.6
  12.4 0.0 copy-start.5
  12.4 0.0 copy-start.4
  12.4 0.6 fusion.15
  13.0 0.0 copy-done.3
  13.1 2.7 %convolution_bitcast_fusion.1 = f32[8,2048]{1,0:T(8,128)} fusion(bf16[4,128,2048]{2,1,0:T(8,128)(2,1)} %param.20, bf16[4,512,128]{2,1,0:T(8,128)(2,1)S(1)} %copy-done.3, bf16[8,4,512]{2,1,0:T(4,128)(2,1)S(1)} %fusion.15), kind=kOutput, calls=%fused_computation.7 | convolution fusion | flops 20975616 | bytes 2719744 | tf_op jit(solution)/shard_map/rhv,hvd->rd/dot_general | solution.py:45
  15.8 0.0 all-reduce.2.cloned.1.call-update
  15.8 0.0 copy-done.6
  15.8 0.1 eq.51
  15.9 0.1 fusion.28
  16.0 0.1 reduce_window_sum.11
  16.0 0.2 select_reduce_fusion
  16.2 0.1 reduce_sum.49
  16.3 0.1 copy.34
  16.4 0.1 convert_reduce_fusion
  16.5 33.2 %all-reduce.2.cloned.1.call-done = f32[8,2048]{1,0:T(8,128)} async-done(((f32[8,2048]{1,0:T(8,128)}), f32[8,2048]{1,0:T(8,128)}) %all-reduce.2.cloned.1.call-update) | async-done | bytes 65552 | tf_op jit(solution)/shard_map/psum | solution.py:88
  49.7 0.0 copy-done.5
  49.7 1.0 multiply_reduce_fusion.1
  50.7 0.0 copy-done.4
  50.7 0.4 convolution_convert_fusion
  51.1 1.1 reshape.86
  52.2 19.0 %all_to_all.10 = bf16[8,8,2,2048]{3,2,1,0:T(2,128)(2,1)S(1)} all-to-all(bf16[8,8,2,2048]{3,2,1,0:T(2,128)(2,1)} %reshape.86), channel_id=1, replica_groups=mesh['ex'=8,'hg'=4] {'ex'}, dimensions={0} | all-to-all | bytes 1048576 | tf_op jit(solution)/shard_map/all_to_all | solution.py:103
  71.2 10.8 %fusion.9 = f32[2,8,8,2,352]{4,1,0,3,2:T(8,128)S(1)} fusion(bf16[8,2,352,2048]{3,2,1,0:T(8,128)(2,1)} %param.24, bf16[8,8,2,2048,1]{3,2,1,0,4:T(2,128)(2,1)S(1)} %bitcast.80), kind=kOutput, calls=%fused_computation.10 | convolution fusion | flops 369098752 | bytes 23953408 | tf_op jit(solution)/shard_map/necd,ejfd->jnecf/dot_general | solution.py:60
  82.0 5.9 %fusion.4 = f32[8,8,2,2048]{3,0,2,1:T(8,128)S(1)} fusion(bf16[8,352,2048]{2,1,0:T(8,128)(2,1)} %param.25, f32[2,8,8,2,352]{4,1,0,3,2:T(8,128)S(1)} %fusion.9), kind=kOutput, calls=%fused_computation.4 | convolution fusion | flops 184819712 | bytes 12943360 | tf_op jit(solution)/shard_map/necf,efd->necd/dot_general | solution.py:62
  87.9 1.9 %copy.38 = f32[8,8,2,2048]{3,2,1,0:T(2,128)} copy(f32[8,8,2,2048]{3,0,2,1:T(8,128)S(1)} %fusion.4) | data formatting | bytes 2097152 | tf_op jit(solution)/shard_map/necf,efd->necd/transpose | solution.py:62
  89.8 4.2 %all-to-all-start.1 = ((f32[8,8,2,2048]{3,2,1,0:T(2,128)}), f32[8,8,2,2048]{3,2,1,0:T(2,128)}, u32[]{:S(2)}, u32[]{:S(2)}) async-start(f32[8,8,2,2048]{3,2,1,0:T(2,128)} %copy.38), calls=%async_computation.1 | async-start | bytes 2097152 | tf_op jit(solution)/shard_map/all_to_all | solution.py:101
  94.0 0.0 reduce-scatter.2.cloned.1.call-start
  94.1 0.0 copy-done
  94.1 0.0 copy-start.2
  94.1 0.9 convolution_bitcast_fusion.2
  95.0 0.5 copy-done.2
  95.4 0.3 convolution_bitcast_fusion
  95.7 0.0 copy-start.7
  95.7 23.3 %all-to-all-done.1 = f32[8,8,2,2048]{3,2,1,0:T(2,128)} async-done(((f32[8,8,2,2048]{3,2,1,0:T(2,128)}), f32[8,8,2,2048]{3,2,1,0:T(2,128)}, u32[]{:S(2)}, u32[]{:S(2)}) %all-to-all-start.1) | async-done | bytes 1048608 | tf_op jit(solution)/shard_map/all_to_all | solution.py:101
  119.0 3.0 %reshape.94 = f32[128,2048,1]{1,0,2:T(8,128)} reshape(f32[8,8,2,2048]{3,2,1,0:T(2,128)} %all-to-all-done.1) | data formatting | bytes 2097152 | tf_op jit(solution)/shard_map/reshape | solution.py:117
  122.0 1.7 %fusion.30 = f32[8,6,2048]{2,0,1:T(8,128)S(1)} fusion(f32[128,2048,1]{1,0,2:T(8,128)} %reshape.94, s32[8,6]{0,1:T(8,128)S(1)} %copy.34), kind=kOutput, calls=%fused_computation.41 | convolution fusion | flops 151001088 | bytes 1441984 | tf_op jit(solution)/shard_map/dot_general | solution.py:118
  123.7 0.8 pad_maximum_fusion
  124.5 0.0 reduce-scatter.2.cloned.1.call-update
  124.6 0.0 copy-done.7
  124.6 0.1 copy.39
  124.7 0.6 dynamic-slice_convert_fusion
  125.3 18.9 %reduce-scatter.2.cloned.1.call-done = f32[8,7,512]{2,0,1:T(8,128)} async-done(((f32[8,7,2048]{2,0,1:T(8,128)}), f32[8,7,512]{2,0,1:T(8,128)}) %reduce-scatter.2.cloned.1.call-update) | async-done | bytes 114704 | tf_op jit(solution)/shard_map/reduce_scatter | solution.py:122
  144.1 0.9 slice.74
  145.0 0.1 multiply_reduce_fusion
  145.1 1.3 fusion.37
  (4 shorter events, 0.0 us)
Async XLA Ops:
  7.2 86.9 %copy-start = (bf16[2,352,2048]{2,1,0:T(8,128)(2,1)S(1)}, bf16[2,352,2048]{2,1,0:T(8,128)(2,1)}, u32[]{:S(2)}) copy-start(bf16[2,352,2048]{2,1,0:T(8,128)(2,1)} %param.26) | copy-start | bytes 8650756
  7.2 42.5 %all-reduce.2.cloned.1.call-start = ((), (), s32[]{:S(2)}) async-start(), calls=%async_computation.3 | async-start | bytes 131072 | tf_op jit(solution)/shard_map/psum | solution.py:88
  7.2 5.1 %copy-start.1 = (bf16[8,240,576]{1,2,0:T(8,128)(2,1)S(1)}, bf16[8,240,576]{1,2,0:T(8,128)(2,1)}, u32[]{:S(2)}) copy-start(bf16[8,240,576]{1,2,0:T(8,128)(2,1)} %param.17) | copy-start | bytes 6635524
  9.9 3.1 %copy-start.3 = (bf16[4,512,128]{2,1,0:T(8,128)(2,1)S(1)}, bf16[4,512,128]{2,1,0:T(8,128)(2,1)}, u32[]{:S(2)}) copy-start(bf16[4,512,128]{2,1,0:T(8,128)(2,1)} %param.19) | copy-start | bytes 1572868
  12.4 3.4 %copy-start.6 = (s32[8,6]{1,0:T(8,128)S(1)}, s32[8,6]{1,0:T(8,128)}, u32[]{:S(2)}) copy-start(s32[8,6]{1,0:T(8,128)} %param.22) | copy-start | bytes 580
  12.4 37.4 %copy-start.5 = (bf16[8,2048]{1,0:T(8,128)(2,1)S(1)}, bf16[8,2048]{1,0:T(8,128)(2,1)}, u32[]{:S(2)}) copy-start(bf16[8,2048]{1,0:T(8,128)(2,1)} %param.14) | copy-start | bytes 98308
  12.4 38.3 %copy-start.4 = (f32[2048]{0:T(1024)S(1)}, f32[2048]{0:T(1024)}, u32[]{:S(2)}) copy-start(f32[2048]{0:T(1024)} %param.21) | copy-start | bytes 24580
  89.8 29.2 %all-to-all-start.1 = ((f32[8,8,2,2048]{3,2,1,0:T(2,128)}), f32[8,8,2,2048]{3,2,1,0:T(2,128)}, u32[]{:S(2)}, u32[]{:S(2)}) async-start(f32[8,8,2,2048]{3,2,1,0:T(2,128)} %copy.38), calls=%async_computation.1 | async-start | bytes 2097152 | tf_op jit(solution)/shard_map/all_to_all | solution.py:101
  94.0 50.1 %reduce-scatter.2.cloned.1.call-start = ((), (), s32[]{:S(2)}) async-start(), calls=%async_computation.4 | async-start | bytes 573440 | tf_op jit(solution)/shard_map/reduce_scatter | solution.py:122
  94.1 1.4 copy-start.2
  95.7 28.8 %copy-start.7 = (f32[8,6]{1,0:T(8,128)S(1)}, f32[8,6]{1,0:T(8,128)}, u32[]{:S(2)}) copy-start(f32[8,6]{1,0:T(8,128)} %param.23) | copy-start | bytes 580
Sparse Core Ops, SparseCore 0:
  15.9 33.7 all-reduce.1
  124.7 19.3 reduce-scatter.1
where the time goes:
time: 154 us; the launch traced here: 153 us
  waiting for transfers between devices  75.4 us (49%)
  matrix products  26.6 us (17%)
  blocking collectives  19 us (12%)
  between operations  14.2 us (9%)
  local copies, waits for them, and re-layouts  8.3 us (5%)
  other arithmetic  5.52 us (4%)
  starting transfers between devices  4.31 us (3%)
    psum x1, waiting for transfers between devices, local(): attn_total = lax.psum(attn_part, 'hg')  33.2 us
    all_to_all x1, waiting for transfers between devices, local(): lax.all_to_all(run_experts(lax.all_to_all(outgoing, 'ex', split_axis=0, c...  23.3 us
    all_to_all x1, blocking collectives, local(): lax.all_to_all(outgoing, 'ex', split_axis=0, concat_axis=0, tiled=True)  19 us
    reduce_scatter x1, waiting for transfers between devices, local(): lax.psum_scatter(stacked, 'hg', scatter_dimension=2, tiled=True)  18.9 us
    dot_general x1, matrix products, run_experts(): jnp.einsum('necd,ejfd->jnecf', arrived, gate_up, preferred_element_type=j...  10.8 us
    dot_general x1, matrix products, run_experts(): jnp.einsum('necf,efd->necd', activation, down_proj, preferred_element_typ...  5.95 us
    all_to_all x1, starting transfers between devices, local(): lax.all_to_all(run_experts(lax.all_to_all(outgoing, 'ex', split_axis=0, c...  4.23 us
  transfers between devices with their start and end apart: 3, of which 3 were waited for; matrix products, arithmetic and copies ran while one was open for 2% of the time, Pallas kernels for 0%

commit v1 on v0

v1 whole, which is shorter than its diff:
```python
import functools

import jax
import jax.numpy as jnp
from jax import lax
from jax.experimental import pallas as pl
from jax.experimental.pallas import tpu as pltpu
from jax.sharding import PartitionSpec as P

LATENT = 512
ROPE = 64
QK_NOPE = 128
EXPERTS = 64
LANES = 128
TILE = 16
MESH = pl.DeviceIdType.MESH

norm_eps = 1e-06


def dot_nt(left, right):
    return lax.dot_general(left, right, (((1,), (1,)), ((), ())), preferred_element_type=jnp.float32)


def dot_nn(left, right):
    return jnp.dot(left, right, preferred_element_type=jnp.float32)


def kernel(
    n_ex,
    n_hg,
    lengths,
    residual,
    queries,
    new_latent,
    gain,
    routes,
    gates,
    cache,
    value_up,
    out_proj,
    gate_up,
    down,
    shared_gate_up,
    shared_down,
    attended_out,
    layer_out,
    kv,
    vu,
    op,
    gu,
    dn,
    sgu,
    sdn,
    mixes,
    attn_part,
    attn_got,
    gate_all,
    x_all,
    x_rows,
    act,
    sact,
    mine,
    part_send,
    part_got,
    row_part,
    row_got,
    hidden,
    kv_sem,
    vu_sem,
    op_sem,
    gu_sem,
    dn_sem,
    sh_sem,
    send_a,
    recv_a,
    send_g,
    recv_g,
    send_x,
    recv_x,
    send_h,
    recv_h,
    send_p,
    recv_p,
    send_r,
    recv_r,
):
    ex = lax.axis_index("ex")
    hg = lax.axis_index("hg")
    rows, slots, keyw = cache.shape
    heads = value_up.shape[0]
    local_experts, _, hidden_units, width = gate_up.shape
    quarter = width // n_hg
    half = quarter // 2
    all_rows = n_ex * rows
    piece = sgu.shape[1]
    pieces = -(-hidden_units // piece)

    kv_copies = [
        pltpu.make_async_copy(cache.at[r], kv.at[r, pl.ds(0, slots)], kv_sem.at[r])
        for r in range(rows)
    ]
    for copy in kv_copies:
        copy.start()
    vu_copy = pltpu.make_async_copy(value_up, vu, vu_sem)
    vu_copy.start()
    op_copy = pltpu.make_async_copy(out_proj, op, op_sem)
    op_copy.start()
    turn = lax.rem(ex, pieces)
    first = pl.multiple_of(
        piece * turn - (pieces * piece - hidden_units) * (turn // max(pieces - 1, 1)), TILE
    )
    sh_copies = [
        pltpu.make_async_copy(shared_gate_up.at[:, pl.ds(first, piece)], sgu, sh_sem.at[0]),
        pltpu.make_async_copy(shared_down.at[pl.ds(first, piece)], sdn, sh_sem.at[1]),
    ]
    for copy in sh_copies:
        copy.start()
    gu_copies = [
        pltpu.make_async_copy(gate_up.at[e], gu.at[e], gu_sem.at[e]) for e in range(local_experts)
    ]
    dn_copies = [
        pltpu.make_async_copy(down.at[e], dn.at[e], dn_sem.at[e]) for e in range(local_experts)
    ]
    for copy in gu_copies + dn_copies:
        copy.start()

    ex_peers = [lax.rem(ex + d, n_ex) for d in range(1, n_ex)]
    hg_peers = [lax.rem(hg + d, n_hg) for d in range(1, n_hg)]
    barrier = pltpu.get_barrier_semaphore()
    for peer in ex_peers:
        pl.semaphore_signal(barrier, inc=1, device_id=(peer, hg), device_id_type=MESH)
    for peer in hg_peers:
        pl.semaphore_signal(barrier, inc=1, device_id=(ex, peer), device_id_type=MESH)

    lane = lax.broadcasted_iota(jnp.int32, (rows, LANES), 1)
    dense = jnp.zeros((rows, LANES), jnp.float32)
    chosen, weight = routes[...], gates[...]
    for k in range(chosen.shape[1]):
        dense += jnp.where(lane == chosen[:, k : k + 1], weight[:, k : k + 1], 0.0)
    gate_all[ex] = dense
    fresh = new_latent[...].astype(jnp.float32)
    top = lax.broadcasted_iota(jnp.int32, (TILE, keyw), 0) == 0
    for r in range(rows):
        kv[r, pl.ds(slots, TILE)] = jnp.where(top, fresh[r : r + 1], 0.0).astype(jnp.bfloat16)

    pl.semaphore_wait(barrier, n_ex - 1 + n_hg - 1)
    gate_copies = []
    for peer in ex_peers:
        copy = pltpu.make_async_remote_copy(
            src_ref=gate_all.at[ex],
            dst_ref=gate_all.at[ex],
            send_sem=send_g.at[peer],
            recv_sem=recv_g.at[ex],
            device_id=(peer, hg),
            device_id_type=MESH,
        )
        copy.start()
        gate_copies.append(copy)

    scale = (QK_NOPE + ROPE) ** (-0.5)
    place = lax.broadcasted_iota(jnp.int32, (heads, slots + TILE), 1)
    for r in range(rows):
        kv_copies[r].wait()
        scores = dot_nt(queries[r], kv[r]) * scale
        usable = (place < lengths[r]) | (place == slots)
        scores = jnp.where(usable, scores, -jnp.inf)
        peak = jnp.max(scores, axis=1, keepdims=True)
        weights = jnp.where(usable, jnp.exp(scores - peak), 0.0)
        probs = (weights / jnp.sum(weights, axis=1, keepdims=True)).astype(jnp.bfloat16)
        mixes[pl.ds(r * heads, heads)] = dot_nn(probs, kv[r, :, :LATENT])
    count = rows * heads
    to_row = lax.broadcasted_iota(jnp.int32, (count, count), 0)
    from_row = lax.broadcasted_iota(jnp.int32, (count, count), 1)
    order = (from_row == lax.rem(to_row, rows) * heads + to_row // rows).astype(jnp.float32)
    by_head = dot_nn(order.astype(jnp.bfloat16), mixes[...].astype(jnp.bfloat16))
    vu_copy.wait()
    head_out = jnp.concatenate(
        [
            dot_nn(by_head[h * rows : (h + 1) * rows].astype(jnp.bfloat16), vu[h])
            for h in range(heads)
        ],
        axis=1,
    ).astype(jnp.bfloat16)
    op_copy.wait()
    proj = op[...].reshape(heads * op.shape[1], width)
    for part in range(n_hg):
        attn_part[part] = dot_nn(head_out, proj[:, part * quarter : (part + 1) * quarter])
    attn_copies = []
    for peer in hg_peers:
        copy = pltpu.make_async_remote_copy(
            src_ref=attn_part.at[peer],
            dst_ref=attn_got.at[hg],
            send_sem=send_a.at[peer],
            recv_sem=recv_a.at[hg],
            device_id=(ex, peer),
            device_id_type=MESH,
        )
        copy.start()
        attn_copies.append(copy)

    def arrived(buffer, peer, sem):
        pltpu.make_async_copy(buffer.at[peer], buffer.at[peer], sem.at[peer]).wait()

    columns = pl.ds(pl.multiple_of(hg * quarter, LANES), quarter)
    state = residual[:, columns].astype(jnp.float32) + attn_part[hg]
    for peer in hg_peers:
        arrived(attn_got, peer, recv_a)
        state += attn_got[peer]
    hidden[...] = state
    attended_out[...] = state.astype(jnp.bfloat16)
    squares = jnp.sum(state * state, axis=1, keepdims=True)
    high = squares.astype(jnp.bfloat16).astype(jnp.float32)
    scaled = state * gain[:, columns]
    packed = jnp.concatenate(
        [
            jnp.concatenate([scaled[:, :half], jnp.broadcast_to(high, (rows, LANES))], axis=1),
            jnp.concatenate(
                [scaled[:, half:], jnp.broadcast_to(squares - high, (rows, LANES))], axis=1
            ),
        ],
        axis=0,
    ).astype(jnp.bfloat16)
    x_all[hg, ex] = packed
    x_copies = []
    for peer in ex_peers:
        copy = pltpu.make_async_remote_copy(
            src_ref=x_all.at[hg, ex],
            dst_ref=x_all.at[hg, ex],
            send_sem=send_x.at[peer],
            recv_sem=recv_x.at[ex],
            device_id=(peer, hg),
            device_id_type=MESH,
        )
        copy.start()
        x_copies.append(copy)
    for peer in ex_peers:
        pltpu.make_async_copy(x_all.at[hg, peer], x_all.at[hg, peer], recv_x.at[peer]).wait()
    h_copies = []
    for peer in hg_peers:
        copy = pltpu.make_async_remote_copy(
            src_ref=x_all.at[hg],
            dst_ref=x_all.at[hg],
            send_sem=send_h.at[peer],
            recv_sem=recv_h.at[hg],
            device_id=(ex, peer),
            device_id_type=MESH,
        )
        copy.start()
        h_copies.append(copy)
    for peer in ex_peers:
        arrived(gate_all, peer, recv_g)
    for peer in hg_peers:
        arrived(x_all, peer, recv_h)

    total = jnp.zeros((all_rows, LANES), jnp.float32)
    for part in range(n_hg):
        block = x_all[part].astype(jnp.float32).reshape(n_ex, 2, rows, half + LANES)
        for side in range(2):
            flat = block[:, side].reshape(all_rows, half + LANES)
            start = part * quarter + side * half
            x_rows[:, start : start + half] = flat[:, :half].astype(jnp.bfloat16)
            total += flat[:, half:]
    inverse = lax.rsqrt(total[:, :1] / width + norm_eps)
    routed = gate_all[...].reshape(all_rows, LANES)
    lanes = lax.broadcasted_iota(jnp.int32, (all_rows, LANES), 1)

    def activate(gate_part, up_part, weight):
        gate_part = gate_part * inverse
        up_part = up_part * inverse
        return (gate_part / (1.0 + jnp.exp(-gate_part)) * up_part * weight).astype(jnp.bfloat16)

    for copy in sh_copies:
        copy.wait()
    unit = first + lax.broadcasted_iota(jnp.int32, (all_rows, piece), 1)
    sact[...] = activate(
        dot_nt(x_rows[...], sgu[0]),
        dot_nt(x_rows[...], sgu[1]),
        jnp.where(unit >= ex * piece, 1.0, 0.0),
    )

    def one_expert(e, carry):
        pltpu.make_async_copy(gate_up.at[e], gu.at[e], gu_sem.at[e]).wait()
        weight = jnp.sum(
            jnp.where(lanes == ex * local_experts + e, routed, 0.0), axis=1, keepdims=True
        )
        act[e] = activate(dot_nt(x_rows[...], gu[e, 0]), dot_nt(x_rows[...], gu[e, 1]), weight)
        return carry

    lax.fori_loop(0, local_experts, one_expert, 0)
    for copy in dn_copies:
        copy.wait()

    def down_part(part):
        where = pl.ds(pl.multiple_of(part * quarter, LANES), quarter)
        return lax.fori_loop(
            0,
            local_experts,
            lambda e, so_far: so_far + dot_nn(act[e], dn[e, :, where]),
            dot_nn(sact[...], sdn[:, where]),
            unroll=True,
        )

    p_copies = []
    for peer in hg_peers:
        part_send[peer] = down_part(peer).astype(jnp.bfloat16)
        copy = pltpu.make_async_remote_copy(
            src_ref=part_send.at[peer],
            dst_ref=part_got.at[hg],
            send_sem=send_p.at[peer],
            recv_sem=recv_p.at[hg],
            device_id=(ex, peer),
            device_id_type=MESH,
        )
        copy.start()
        p_copies.append(copy)
    mine[...] = down_part(hg)
    for peer in hg_peers:
        arrived(part_got, peer, recv_p)
    summed = mine[...]
    for peer in hg_peers:
        summed += part_got[peer].astype(jnp.float32)
    row_part[...] = summed.reshape(n_ex, rows, quarter)
    r_copies = []
    for peer in ex_peers:
        copy = pltpu.make_async_remote_copy(
            src_ref=row_part.at[peer],
            dst_ref=row_got.at[ex],
            send_sem=send_r.at[peer],
            recv_sem=recv_r.at[ex],
            device_id=(peer, hg),
            device_id_type=MESH,
        )
        copy.start()
        r_copies.append(copy)
    final = hidden[...] + row_part[ex]
    for peer in ex_peers:
        arrived(row_got, peer, recv_r)
        final += row_got[peer]
    layer_out[...] = final.astype(jnp.bfloat16)
    for copy in gate_copies + attn_copies + x_copies + h_copies + p_copies + r_copies:
        copy.wait_send()


def local(
    residual_in,
    queries,
    new_latent,
    cache,
    lengths,
    value_up,
    out_proj,
    norm_gain,
    routes,
    gate_weights,
    expert_gate_up,
    expert_down,
    shared_gate_up,
    shared_down,
):
    n_ex, n_hg = lax.axis_size("ex"), lax.axis_size("hg")
    rows, slots, keyw = cache.shape
    heads, _, head_v = value_up.shape
    local_experts, _, units, width = expert_gate_up.shape
    quarter = width // n_hg
    piece = -(-(units // TILE) // n_ex) * TILE
    bf16, f32 = jnp.bfloat16, jnp.float32
    vmem, dma = pltpu.VMEM, pltpu.SemaphoreType.DMA
    in_vmem, in_hbm = pl.BlockSpec(memory_space=pltpu.VMEM), pl.BlockSpec(memory_space=pl.ANY)
    out = jax.ShapeDtypeStruct((rows, quarter), bf16)
    return pl.pallas_call(
        functools.partial(kernel, n_ex, n_hg),
        out_shape=(out, out),
        in_specs=[pl.BlockSpec(memory_space=pltpu.SMEM)] + [in_vmem] * 6 + [in_hbm] * 7,
        out_specs=(in_vmem, in_vmem),
        scratch_shapes=[
            vmem((rows, slots + TILE, keyw), bf16),
            vmem(value_up.shape, bf16),
            vmem(out_proj.shape, bf16),
            vmem(expert_gate_up.shape, bf16),
            vmem(expert_down.shape, bf16),
            vmem((2, piece, width), bf16),
            vmem((piece, width), bf16),
            vmem((rows * heads, LATENT), f32),
            vmem((n_hg, rows, quarter), f32),
            vmem((n_hg, rows, quarter), f32),
            vmem((n_ex, rows, LANES), f32),
            vmem((n_hg, n_ex, 2 * rows, quarter // 2 + LANES), bf16),
            vmem((n_ex * rows, width), bf16),
            vmem((local_experts, n_ex * rows, units), bf16),
            vmem((n_ex * rows, piece), bf16),
            vmem((n_ex * rows, quarter), f32),
            vmem((n_hg, n_ex * rows, quarter), bf16),
            vmem((n_hg, n_ex * rows, quarter), bf16),
            vmem((n_ex, rows, quarter), f32),
            vmem((n_ex, rows, quarter), f32),
            vmem((rows, quarter), f32),
            dma((rows,)),
            dma,
            dma,
            dma((local_experts,)),
            dma((local_experts,)),
            dma((2,)),
            dma((n_hg,)),
            dma((n_hg,)),
            dma((n_ex,)),
            dma((n_ex,)),
            dma((n_ex,)),
            dma((n_ex,)),
            dma((n_hg,)),
            dma((n_hg,)),
            dma((n_hg,)),
            dma((n_hg,)),
            dma((n_ex,)),
            dma((n_ex,)),
        ],
        compiler_params=pltpu.CompilerParams(
            collective_id=0, has_side_effects=True, vmem_limit_bytes=58 * 1024 * 1024
        ),
    )(
        lengths,
        residual_in,
        queries,
        new_latent,
        norm_gain.reshape(1, -1),
        routes,
        gate_weights,
        cache,
        value_up,
        out_proj,
        expert_gate_up,
        expert_down,
        shared_gate_up,
        shared_down,
    )


def solution(mesh):
    placed = (
        P("ex", None),
        P("ex", "hg", None),
        P("ex", None),
        P("ex", None, None),
        P("ex"),
        P("hg", None, None),
        P("hg", None, None),
        P(),
        P("ex", None),
        P("ex", None),
        P("ex", None, "hg", None),
        P("ex", "hg", None),
        P(None, "hg", None),
        P("hg", None),
    )
    return jax.shard_map(
        local, mesh=mesh, in_specs=placed, out_specs=(P("ex", "hg"), P("ex", "hg")), check_vma=False
    )
```

time: 154 us -> 54.4 us (0.35)
  waiting for transfers between devices: 75.4 us -> 0 us
  Pallas kernels: 0 us -> 46.5 us
  matrix products: 26.6 us -> 0 us
  blocking collectives: 19 us -> 0 us
  between operations: 14.2 us -> 0.64 us
  other arithmetic: 5.52 us -> 0 us
  starting transfers between devices: 4.31 us -> 0 us
    pallas_call x0 -> x1, Pallas kernels: none -> 46.5 us  [local(): pl.pallas_call(functools.partial(kernel, n_ex, n_hg), out_shape=(out, out...]
    psum x1 -> x0, waiting for transfers between devices: 33.2 us -> none  [local(): attn_total = lax.psum(attn_part, 'hg')]
    dot_general x10 -> x0, matrix products: 26.6 us -> none  [the longest x1 10.8 us: run_experts(): jnp.einsum('necd,ejfd->jnecf', arrived, gate_up, preferred_element_type=j...]
    all_to_all x1 -> x0, waiting for transfers between devices: 23.3 us -> none  [local(): lax.all_to_all(run_experts(lax.all_to_all(outgoing, 'ex', split_axis=0, c...]
    all_to_all x1 -> x0, blocking collectives: 19 us -> none  [local(): lax.all_to_all(outgoing, 'ex', split_axis=0, concat_axis=0, tiled=True)]
    reduce_scatter x1 -> x0, waiting for transfers between devices: 18.9 us -> none  [local(): lax.psum_scatter(stacked, 'hg', scatter_dimension=2, tiled=True)]
    unnamed x17 -> x3, local copies, waits for them, and re-layouts: 0.6 us -> 6.9 us
    all_to_all x1 -> x0, starting transfers between devices: 4.23 us -> none  [local(): lax.all_to_all(run_experts(lax.all_to_all(outgoing, 'ex', split_axis=0, c...]
  transfers between devices with their start and end apart: 3 -> 0, of which waited for: 3 -> 0; matrix products, arithmetic and copies ran while one was open for 2% -> 0% of each run, Pallas kernels for 0% -> 0%
where the time goes in v1:
time: 54.4 us; the launch traced here: 54.1 us
  Pallas kernels  46.5 us (85%)
  local copies, waits for them, and re-layouts  6.9 us (13%)
  between operations  0.64 us (1%)
    pallas_call x1, Pallas kernels, local(): pl.pallas_call(functools.partial(kernel, n_ex, n_hg), out_shape=(out, out...  46.5 us
    unnamed x3, local copies, waits for them, and re-layouts  6.9 us

profile of v1, /device:TPU:0, one launch (start us, length us, event | category | flops | bytes accessed | tf_op | source)
XLA Modules:
  0.0 54.1 jit_solution(3870356843676064460)
XLA Ops:
  0.6 4.3 %copy.16.cache = bf16[8,240,576]{2,1,0:T(8,128)(2,1)} copy(bf16[8,240,576]{1,2,0:T(8,128)(2,1)} %param.17) | data formatting | bytes 4423680 | tf_op args[3]
  4.9 46.5 %shard_map.149 = (bf16[8,512]{1,0:T(8,128)(2,1)}, bf16[8,512]{1,0:T(8,128)(2,1)}) custom-call(s32[8]{0:T(128)} %lengths.1, bf16[8,2048]{1,0:T(8,128)(2,1)} %residual.1, bf16[8,4,576]{2,1,0:T(4,128)(2,1)} %queries.1, bf16[8,576]{1,0:T(8,128)(2,1)} %new_latent.1, f32[1,2048]{1,0:T(1,128)} %bitcast.1, s32[8,6]{1,0:T(8,128)} %routes.1, f32[8,6]{1,0:T(8,128)} %gates.1, ...), custom_call_target="tpu_custom_call" | custom-call | tf_op jit(solution)/shard_map/pallas_call | solution.py:371
  51.5 1.3 %copy.19 = bf16[8,512]{1,0:T(8,128)(2,1)} copy(bf16[8,512]{1,0:T(8,128)(2,1)} %get-tuple-element.4) | data formatting | bytes 16384
  52.8 1.3 %copy.20 = bf16[8,512]{1,0:T(8,128)(2,1)} copy(bf16[8,512]{1,0:T(8,128)(2,1)} %get-tuple-element.5) | data formatting | bytes 16384

commit v2 on v1

--- a/solution.py
+++ b/solution.py
@@ -43,8 +43,7 @@
     down,
     shared_gate_up,
     shared_down,
-    attended_out,
-    layer_out,
+    outs,
     kv,
     vu,
     op,
@@ -58,6 +57,8 @@
     gate_all,
     x_all,
     x_rows,
+    pairs,
+    spairs,
     act,
     sact,
     mine,
@@ -87,7 +88,7 @@
 ):
     ex = lax.axis_index("ex")
     hg = lax.axis_index("hg")
-    rows, slots, keyw = cache.shape
+    rows, _, slots = cache.shape
     heads = value_up.shape[0]
     local_experts, _, hidden_units, width = gate_up.shape
     quarter = width // n_hg
@@ -97,7 +98,7 @@
     pieces = -(-hidden_units // piece)
 
     kv_copies = [
-        pltpu.make_async_copy(cache.at[r], kv.at[r, pl.ds(0, slots)], kv_sem.at[r])
+        pltpu.make_async_copy(cache.at[r], kv.at[r], kv_sem.at[r])
         for r in range(rows)
     ]
     for copy in kv_copies:
@@ -122,11 +123,17 @@
     dn_copies = [
         pltpu.make_async_copy(down.at[e], dn.at[e], dn_sem.at[e]) for e in range(local_experts)
     ]
-    for copy in gu_copies + dn_copies:
+    early = local_experts * 3 // 8
+    for copy in gu_copies[:early]:
         copy.start()
 
     ex_peers = [lax.rem(ex + d, n_ex) for d in range(1, n_ex)]
-    hg_peers = [lax.rem(hg + d, n_hg) for d in range(1, n_hg)]
+    pair = 2 - n_hg % 2
+    hg_peers = []
+    for d in range(0, n_hg, pair):
+        base = lax.rem(hg + d, n_hg)
+        other = base + 1 - 2 * lax.rem(base, 2)
+        hg_peers += ([base] if d else []) + ([other] if pair == 2 else [])
     barrier = pltpu.get_barrier_semaphore()
     for peer in ex_peers:
         pl.semaphore_signal(barrier, inc=1, device_id=(peer, hg), device_id_type=MESH)
@@ -139,10 +146,6 @@
     for k in range(chosen.shape[1]):
         dense += jnp.where(lane == chosen[:, k : k + 1], weight[:, k : k + 1], 0.0)
     gate_all[ex] = dense
-    fresh = new_latent[...].astype(jnp.float32)
-    top = lax.broadcasted_iota(jnp.int32, (TILE, keyw), 0) == 0
-    for r in range(rows):
-        kv[r, pl.ds(slots, TILE)] = jnp.where(top, fresh[r : r + 1], 0.0).astype(jnp.bfloat16)
 
     pl.semaphore_wait(barrier, n_ex - 1 + n_hg - 1)
     gate_copies = []
@@ -159,16 +162,25 @@
         gate_copies.append(copy)
 
     scale = (QK_NOPE + ROPE) ** (-0.5)
-    place = lax.broadcasted_iota(jnp.int32, (heads, slots + TILE), 1)
+    fresh = new_latent[...].astype(jnp.float32)
+    place = lax.broadcasted_iota(jnp.int32, (heads, slots), 1)
     for r in range(rows):
+        own = (
+            jnp.sum(queries[r].astype(jnp.float32) * fresh[r : r + 1], axis=1, keepdims=True)
+            * scale
+        )
         kv_copies[r].wait()
-        scores = dot_nt(queries[r], kv[r]) * scale
-        usable = (place < lengths[r]) | (place == slots)
-        scores = jnp.where(usable, scores, -jnp.inf)
-        peak = jnp.max(scores, axis=1, keepdims=True)
+        usable = place < lengths[r]
+        scores = jnp.where(usable, dot_nn(queries[r], kv[r]) * scale, -jnp.inf)
+        peak = jnp.maximum(jnp.max(scores, axis=1, keepdims=True), own)
         weights = jnp.where(usable, jnp.exp(scores - peak), 0.0)
-        probs = (weights / jnp.sum(weights, axis=1, keepdims=True)).astype(jnp.bfloat16)
-        mixes[pl.ds(r * heads, heads)] = dot_nn(probs, kv[r, :, :LATENT])
+        weight_own = jnp.exp(own - peak)
+        share = 1.0 / (jnp.sum(weights, axis=1, keepdims=True) + weight_own)
+        probs = (weights * share).astype(jnp.bfloat16)
+        probs_own = (weight_own * share).astype(jnp.bfloat16).astype(jnp.float32)
+        mixes[pl.ds(r * heads, heads)] = (
+            dot_nt(probs, kv[r, :LATENT]) + probs_own * fresh[r : r + 1, :LATENT]
+        )
     count = rows * heads
     to_row = lax.broadcasted_iota(jnp.int32, (count, count), 0)
     from_row = lax.broadcasted_iota(jnp.int32, (count, count), 1)
@@ -198,6 +210,8 @@
         )
         copy.start()
         attn_copies.append(copy)
+    for copy in gu_copies[early:]:
+        copy.start()
 
     def arrived(buffer, peer, sem):
         pltpu.make_async_copy(buffer.at[peer], buffer.at[peer], sem.at[peer]).wait()
@@ -208,7 +222,7 @@
         arrived(attn_got, peer, recv_a)
         state += attn_got[peer]
     hidden[...] = state
-    attended_out[...] = state.astype(jnp.bfloat16)
+    outs[0] = state
     squares = jnp.sum(state * state, axis=1, keepdims=True)
     high = squares.astype(jnp.bfloat16).astype(jnp.float32)
     scaled = state * gain[:, columns]
@@ -248,19 +262,35 @@
         )
         copy.start()
         h_copies.append(copy)
+    for copy in dn_copies:
+        copy.start()
     for peer in ex_peers:
         arrived(gate_all, peer, recv_g)
-    for peer in hg_peers:
-        arrived(x_all, peer, recv_h)
-
+
+    for copy in sh_copies + gu_copies:
+        copy.wait()
     total = jnp.zeros((all_rows, LANES), jnp.float32)
-    for part in range(n_hg):
+    for number, part in enumerate([hg] + hg_peers):
+        if number:
+            arrived(x_all, part, recv_h)
         block = x_all[part].astype(jnp.float32).reshape(n_ex, 2, rows, half + LANES)
-        for side in range(2):
-            flat = block[:, side].reshape(all_rows, half + LANES)
-            start = part * quarter + side * half
-            x_rows[:, start : start + half] = flat[:, :half].astype(jnp.bfloat16)
-            total += flat[:, half:]
+        sides = [block[:, side].reshape(all_rows, half + LANES) for side in range(2)]
+        x_rows[:, :half] = sides[0][:, :half].astype(jnp.bfloat16)
+        x_rows[:, half:] = sides[1][:, :half].astype(jnp.bfloat16)
+        total += sides[0][:, half:] + sides[1][:, half:]
+        where = pl.ds(pl.multiple_of(part * quarter, LANES), quarter)
+        values = x_rows[...]
+        for j in range(2):
+            product = dot_nt(values, sgu[j, :, where])
+            spairs[j] = product if number == 0 else spairs[j] + product
+
+        def one_expert(e, carry):
+            for j in range(2):
+                product = dot_nt(values, gu[e, j, :, where])
+                pairs[e, j] = product if number == 0 else pairs[e, j] + product
+            return carry
+
+        lax.fori_loop(0, local_experts, one_expert, 0, unroll=True)
     inverse = lax.rsqrt(total[:, :1] / width + norm_eps)
     routed = gate_all[...].reshape(all_rows, LANES)
     lanes = lax.broadcasted_iota(jnp.int32, (all_rows, LANES), 1)
@@ -270,24 +300,17 @@
         up_part = up_part * inverse
         return (gate_part / (1.0 + jnp.exp(-gate_part)) * up_part * weight).astype(jnp.bfloat16)
 
-    for copy in sh_copies:
-        copy.wait()
     unit = first + lax.broadcasted_iota(jnp.int32, (all_rows, piece), 1)
-    sact[...] = activate(
-        dot_nt(x_rows[...], sgu[0]),
-        dot_nt(x_rows[...], sgu[1]),
-        jnp.where(unit >= ex * piece, 1.0, 0.0),
-    )
-
-    def one_expert(e, carry):
-        pltpu.make_async_copy(gate_up.at[e], gu.at[e], gu_sem.at[e]).wait()
+    sact[...] = activate(spairs[0], spairs[1], jnp.where(unit >= ex * piece, 1.0, 0.0))
+
+    def finish_expert(e, carry):
         weight = jnp.sum(
             jnp.where(lanes == ex * local_experts + e, routed, 0.0), axis=1, keepdims=True
         )
-        act[e] = activate(dot_nt(x_rows[...], gu[e, 0]), dot_nt(x_rows[...], gu[e, 1]), weight)
+        act[e] = activate(pairs[e, 0], pairs[e, 1], weight)
         return carry
 
-    lax.fori_loop(0, local_experts, one_expert, 0)
+    lax.fori_loop(0, local_experts, finish_expert, 0)
     for copy in dn_copies:
         copy.wait()
 
@@ -337,7 +360,7 @@
     for peer in ex_peers:
         arrived(row_got, peer, recv_r)
         final += row_got[peer]
-    layer_out[...] = final.astype(jnp.bfloat16)
+    outs[1] = final
     for copy in gate_copies + attn_copies + x_copies + h_copies + p_copies + r_copies:
         copy.wait_send()
 
@@ -367,14 +390,13 @@
     bf16, f32 = jnp.bfloat16, jnp.float32
     vmem, dma = pltpu.VMEM, pltpu.SemaphoreType.DMA
     in_vmem, in_hbm = pl.BlockSpec(memory_space=pltpu.VMEM), pl.BlockSpec(memory_space=pl.ANY)
-    out = jax.ShapeDtypeStruct((rows, quarter), bf16)
-    return pl.pallas_call(
+    outs = pl.pallas_call(
         functools.partial(kernel, n_ex, n_hg),
-        out_shape=(out, out),
+        out_shape=jax.ShapeDtypeStruct((2, rows, quarter), f32),
         in_specs=[pl.BlockSpec(memory_space=pltpu.SMEM)] + [in_vmem] * 6 + [in_hbm] * 7,
-        out_specs=(in_vmem, in_vmem),
+        out_specs=in_vmem,
         scratch_shapes=[
-            vmem((rows, slots + TILE, keyw), bf16),
+            vmem((rows, keyw, slots), bf16),
             vmem(value_up.shape, bf16),
             vmem(out_proj.shape, bf16),
             vmem(expert_gate_up.shape, bf16),
@@ -386,7 +408,9 @@
             vmem((n_hg, rows, quarter), f32),
             vmem((n_ex, rows, LANES), f32),
             vmem((n_hg, n_ex, 2 * rows, quarter // 2 + LANES), bf16),
-            vmem((n_ex * rows, width), bf16),
+            vmem((n_ex * rows, quarter), bf16),
+            vmem((local_experts, 2, n_ex * rows, units), f32),
+            vmem((2, n_ex * rows, piece), f32),
             vmem((local_experts, n_ex * rows, units), bf16),
             vmem((n_ex * rows, piece), bf16),
             vmem((n_ex * rows, quarter), f32),
@@ -425,7 +449,7 @@
         norm_gain.reshape(1, -1),
         routes,
         gate_weights,
-        cache,
+        jnp.swapaxes(cache, 1, 2),
         value_up,
         out_proj,
         expert_gate_up,
@@ -433,6 +457,7 @@
         shared_gate_up,
         shared_down,
     )
+    return outs[0].astype(bf16), outs[1].astype(bf16)
 
 
 def solution(mesh):

time: 54.4 us -> 41 us (0.75)
  Pallas kernels: 46.5 us -> 38.7 us
  local copies, waits for them, and re-layouts: 6.9 us -> 0.61 us
  other arithmetic: 0 us -> 0.76 us
    pallas_call x1, Pallas kernels: 46.5 us -> 38.7 us  [local(): pl.pallas_call(functools.partial(kernel, n_ex, n_hg), out_shape=jax.Shape...]
    unnamed x3 -> x0, local copies, waits for them, and re-layouts: 6.9 us -> none
    another operation x0 -> x1, other arithmetic: none -> 0.76 us
    convert_element_type x0 -> x1, local copies, waits for them, and re-layouts: none -> 0.61 us  [local(): return (outs[0].astype(bf16), outs[1].astype(bf16))]
where the time goes in v2:
time: 41 us; the launch traced here: 40.7 us
  Pallas kernels  38.7 us (94%)
  other arithmetic  0.76 us (2%)
  between operations  0.64 us (2%)
  local copies, waits for them, and re-layouts  0.61 us (1%)
    pallas_call x1, Pallas kernels, local(): pl.pallas_call(functools.partial(kernel, n_ex, n_hg), out_shape=jax.Shape...  38.7 us

profile of v2, /device:TPU:0, one launch (start us, length us, event | category | flops | bytes accessed | tf_op | source)
XLA Modules:
  0.0 40.7 jit_solution(16936166285683735890)
XLA Ops:
  0.6 38.7 %shard_map.149 = f32[2,8,512]{2,1,0:T(8,128)} custom-call(s32[8]{0:T(128)} %lengths.1, bf16[8,2048]{1,0:T(8,128)(2,1)} %residual.1, bf16[8,4,576]{2,1,0:T(4,128)(2,1)} %queries.1, bf16[8,576]{1,0:T(8,128)(2,1)} %new_latent.1, f32[1,2048]{1,0:T(1,128)} %bitcast.7, s32[8,6]{1,0:T(8,128)} %routes.1, f32[8,6]{1,0:T(8,128)} %gates.1, ...), custom_call_target="tpu_custom_call" | custom-call | tf_op jit(solution)/shard_map/pallas_call | solution.py:393
  39.3 0.8 %convert.4 = bf16[2,8,512]{2,1,0:T(8,128)(2,1)S(1)} convert(f32[2,8,512]{2,1,0:T(8,128)} %shard_map.149) | non-fusion elementwise | flops 8192 | bytes 49152 | tf_op jit(solution)/shard_map/convert.1
  40.1 0.6 %slice_bitcast_fusion = (bf16[8,512]{1,0:T(8,128)(2,1)}, bf16[8,512]{1,0:T(8,128)(2,1)}) fusion(bf16[2,8,512]{2,1,0:T(8,128)(2,1)S(1)} %convert.4), kind=kLoop, calls=%fused_computation | loop fusion | bytes 32768 | tf_op jit(solution)/shard_map/convert_element_type | solution.py:460

commit v3 on v2

--- a/solution.py
+++ b/solution.py
@@ -195,11 +195,14 @@
         axis=1,
     ).astype(jnp.bfloat16)
     op_copy.wait()
-    proj = op[...].reshape(heads * op.shape[1], width)
-    for part in range(n_hg):
-        attn_part[part] = dot_nn(head_out, proj[:, part * quarter : (part + 1) * quarter])
+
+    def project(part):
+        where = pl.ds(pl.multiple_of(part * quarter, LANES), quarter)
+        attn_part[part] = dot_nn(head_out, op[:, :, where].reshape(heads * op.shape[1], quarter))
+
     attn_copies = []
-    for peer in hg_peers:
+    for peer in hg_peers[::-1]:
+        project(peer)
         copy = pltpu.make_async_remote_copy(
             src_ref=attn_part.at[peer],
             dst_ref=attn_got.at[hg],
@@ -210,6 +213,7 @@
         )
         copy.start()
         attn_copies.append(copy)
+    project(hg)
     for copy in gu_copies[early:]:
         copy.start()
 
@@ -251,17 +255,22 @@
     for peer in ex_peers:
         pltpu.make_async_copy(x_all.at[hg, peer], x_all.at[hg, peer], recv_x.at[peer]).wait()
     h_copies = []
-    for peer in hg_peers:
-        copy = pltpu.make_async_remote_copy(
-            src_ref=x_all.at[hg],
-            dst_ref=x_all.at[hg],
-            send_sem=send_h.at[peer],
-            recv_sem=recv_h.at[hg],
+
+    def share(part, peer, slot):
+        copy = pltpu.make_async_remote_copy(
+            src_ref=x_all.at[part],
+            dst_ref=x_all.at[part],
+            send_sem=send_h.at[slot],
+            recv_sem=recv_h.at[part],
             device_id=(ex, peer),
             device_id_type=MESH,
         )
         copy.start()
         h_copies.append(copy)
+
+    relay = n_hg == 4
+    for peer in (hg_peers[1::-1] if relay else hg_peers):
+        share(hg, peer, peer)
     for copy in dn_copies:
         copy.start()
     for peer in ex_peers:
@@ -273,6 +282,8 @@
     for number, part in enumerate([hg] + hg_peers):
         if number:
             arrived(x_all, part, recv_h)
+        if relay and number == 2:
+            share(part, hg_peers[0], hg_peers[2])
         block = x_all[part].astype(jnp.float32).reshape(n_ex, 2, rows, half + LANES)
         sides = [block[:, side].reshape(all_rows, half + LANES) for side in range(2)]
         x_rows[:, :half] = sides[0][:, :half].astype(jnp.bfloat16)
@@ -325,7 +336,7 @@
         )
 
     p_copies = []
-    for peer in hg_peers:
+    for peer in hg_peers[::-1]:
         part_send[peer] = down_part(peer).astype(jnp.bfloat16)
         copy = pltpu.make_async_remote_copy(
             src_ref=part_send.at[peer],

time: 41 us -> 40.2 us (0.980)
  Pallas kernels: 38.7 us -> 37.9 us
    pallas_call x1, Pallas kernels: 38.7 us -> 37.9 us  [local(): pl.pallas_call(functools.partial(kernel, n_ex, n_hg), out_shape=jax.Shape...]
where the time goes in v3:
time: 40.2 us; the launch traced here: 39.9 us
  Pallas kernels  37.9 us (94%)
  other arithmetic  0.76 us (2%)
  between operations  0.64 us (2%)
  local copies, waits for them, and re-layouts  0.61 us (2%)
    pallas_call x1, Pallas kernels, local(): pl.pallas_call(functools.partial(kernel, n_ex, n_hg), out_shape=jax.Shape...  37.9 us

profile of v3, /device:TPU:0, one launch (start us, length us, event | category | flops | bytes accessed | tf_op | source)
XLA Modules:
  0.0 39.9 jit_solution(6691542360097726627)
XLA Ops:
  0.6 37.9 %shard_map.149 = f32[2,8,512]{2,1,0:T(8,128)} custom-call(s32[8]{0:T(128)} %lengths.1, bf16[8,2048]{1,0:T(8,128)(2,1)} %residual.1, bf16[8,4,576]{2,1,0:T(4,128)(2,1)} %queries.1, bf16[8,576]{1,0:T(8,128)(2,1)} %new_latent.1, f32[1,2048]{1,0:T(1,128)} %bitcast.7, s32[8,6]{1,0:T(8,128)} %routes.1, f32[8,6]{1,0:T(8,128)} %gates.1, ...), custom_call_target="tpu_custom_call" | custom-call | tf_op jit(solution)/shard_map/pallas_call | solution.py:404
  38.5 0.8 %convert.4 = bf16[2,8,512]{2,1,0:T(8,128)(2,1)S(1)} convert(f32[2,8,512]{2,1,0:T(8,128)} %shard_map.149) | non-fusion elementwise | flops 8192 | bytes 49152 | tf_op jit(solution)/shard_map/convert.1
  39.3 0.6 %slice_bitcast_fusion = (bf16[8,512]{1,0:T(8,128)(2,1)}, bf16[8,512]{1,0:T(8,128)(2,1)}) fusion(bf16[2,8,512]{2,1,0:T(8,128)(2,1)S(1)} %convert.4), kind=kLoop, calls=%fused_computation | loop fusion | bytes 32768 | tf_op jit(solution)/shard_map/convert_element_type | solution.py:471
